TPU v7x, 256 devices: a whole 4x4x8 slice. The times are simulated.
256 devices in a mesh: sky: 64 (over z, y, core), batch: 4 (over x).
Axes of the slice: x: 4, y: 4, z: 8, core: 2. Of those that a mesh axis runs over, the one named last changes fastest.
Arguments:
- features: float32 [4, 64, 80, 1024], P('batch', 'sky'), may hold values from -0.1875 to 0.1875
- target: float32 [4, 64, 576, 1024], P('batch', 'sky'), may hold values from -2 to 2
- images: float32 [4, 64, 16, 80], P('batch', 'sky'), may hold values from -6 to 6
- layer_mask: int32 [4, 64, 16], P('batch', 'sky'), may hold values 0 or 1
- pair_list: int32 [4, 64, 9], P('batch', 'sky'), may hold values from 0 to 11, as said below
- ridge_weight: float32 [4, 64], P('batch', 'sky'), may hold values from 0.2 to 1
Outputs:
- transfer: float32 [4, 64, 720, 576], P('batch', 'sky')
- final_image: float32 [16, 96, 1536], P(None, 'batch', 'sky')
Inputs may be any that keep to these rules, and one draw needn't show every extreme that they name: `pair_list`: the 9 entries of each output stamp are distinct candidate numbers.
All inputs are finite; a program needn't handle non-finite values. No bound on the sum of `layer_mask` on one device may be relied on, other than what follows from the above.
Results may differ from a plain program's by a relative error of at most 0.0003.
Values sent between devices are 32-bit elements; how exact they have to be, the bound alone decides.
A program may use at most 128 MiB of HBM per device.

v0:
```python
import functools

import jax
import jax.numpy as jnp
from jax import lax
from jax.experimental import pallas as pl
from jax.experimental.pallas import tpu as pltpu
from jax.sharding import PartitionSpec as P

NPIX = 80
FEAT = 1024
SIDE = 24
LAYERS = 16
NSEL = 9
FADE = 4
ORDER = 720
NOUT_PIX = 576
CAND = 12

TILE = 128
NBLOCK = 6
PADDED = TILE * NBLOCK
HALF = NPIX // 2
MESH = pl.DeviceIdType.MESH
HIGH = lax.Precision.HIGH
F32 = jnp.float32
BF16 = jnp.bfloat16


def gather_kernel(
    n_sky, n_batch, feat_ref, image_ref, mask_ref, window_ref, stamps_ref,
    masked, zeros, zero_image, local_sem, fs_sem, fr_sem, ys_sem, yr_sem, is_sem, ir_sem, js_sem, jr_sem,
):
    s = lax.axis_index("sky")
    b = lax.axis_index("batch")
    up = lax.rem(s + 1, n_sky)
    down = lax.rem(s + n_sky - 1, n_sky)
    right = lax.rem(b + 1, n_batch)
    left = lax.rem(b + n_batch - 1, n_batch)
    far = lax.rem(b + 2, n_batch)

    barrier = pltpu.get_barrier_semaphore()
    for where in ((s, left), (s, right), (up, b), (down, b)):
        pl.semaphore_signal(barrier, inc=1, device_id=where, device_id_type=MESH)

    row = lax.broadcasted_iota(jnp.int32, (LAYERS, NPIX), 0)
    keep = jnp.zeros((LAYERS, NPIX), jnp.int32)
    for layer in range(LAYERS):
        keep = jnp.where(row == layer, mask_ref[layer], keep)
    masked[...] = jnp.zeros((LAYERS, TILE), F32)
    masked[:, :NPIX] = image_ref[...] * keep.astype(F32)
    zeros[...] = jnp.zeros((NPIX, FEAT), F32)
    zero_image[...] = jnp.zeros((LAYERS, TILE), F32)

    pl.semaphore_wait(barrier, 4)

    rows = (pl.ds(0, HALF), pl.ds(HALF, HALF))

    def remote(src, dst, send, recv, where):
        return pltpu.make_async_remote_copy(
            src_ref=src, dst_ref=dst, send_sem=send, recv_sem=recv, device_id=where, device_id_type=MESH
        )

    def along(number, owner, half, where, src=None):
        slot = window_ref.at[3 * owner + 1, rows[half]]
        return remote(slot if src is None else src, slot, fs_sem.at[number], fr_sem.at[number], where)

    own_half = (feat_ref.at[rows[0]], feat_ref.at[rows[1]])
    sends = []
    for half in (0, 1):
        sends += [
            along(0 + half, b, half, (s, right), own_half[half]),
            along(2 + half, b, half, (s, left), own_half[half]),
        ]
        for copy in sends[-2:]:
            copy.start()

    def across(place, owner, half, src=None):
        base = window_ref.at[3 * owner + 1, rows[half]] if src is None else src
        number = 2 * place + half
        return (
            remote(base, window_ref.at[3 * owner, rows[half]], ys_sem.at[0, number], yr_sem.at[0, number], (up, b)),
            remote(base, window_ref.at[3 * owner + 2, rows[half]], ys_sem.at[1, number], yr_sem.at[1, number], (down, b)),
        )

    def start(copies):
        for copy in copies:
            copy.start()
        sends.extend(copies)

    for half in (0, 1):
        start(across(0, b, half, own_half[half]))

    own = [
        pltpu.make_async_copy(feat_ref, window_ref.at[3 * b + 1], local_sem.at[0]),
        pltpu.make_async_copy(masked, stamps_ref.at[3 * b + 1], local_sem.at[1]),
    ]
    for copy in own:
        copy.start()

    def image_along(number, owner, where, src):
        return remote(src, stamps_ref.at[3 * owner + 1], is_sem.at[number], ir_sem.at[number], where)

    def image_across(place, owner, src):
        return (
            remote(src, stamps_ref.at[3 * owner], js_sem.at[0, place], jr_sem.at[0, place], (up, b)),
            remote(src, stamps_ref.at[3 * owner + 2], js_sem.at[1, place], jr_sem.at[1, place], (down, b)),
        )

    start((image_along(0, b, (s, right), masked), image_along(1, b, (s, left), masked)))
    start(image_across(0, b, masked))

    along(0, left, 0, (s, left)).wait_recv()
    start((along(4, left, 0, (s, right)),))
    start(across(1, left, 0))
    along(2, right, 0, (s, right)).wait_recv()
    start(across(2, right, 0))
    along(3, right, 1, (s, right)).wait_recv()
    start((along(5, right, 1, (s, left)),))
    start(across(2, right, 1))
    along(1, left, 1, (s, left)).wait_recv()
    start(across(1, left, 1))

    image_along(0, left, (s, left), stamps_ref.at[3 * left + 1]).wait_recv()
    start((image_along(2, left, (s, right), stamps_ref.at[3 * left + 1]),))
    start(image_across(1, left, stamps_ref.at[3 * left + 1]))
    image_along(1, right, (s, right), stamps_ref.at[3 * right + 1]).wait_recv()
    start(image_across(2, right, stamps_ref.at[3 * right + 1]))
    image_along(2, far, (s, left), stamps_ref.at[3 * far + 1]).wait_recv()
    start(image_across(3, far, stamps_ref.at[3 * far + 1]))

    along(4, far, 0, (s, left)).wait_recv()
    start(across(3, far, 0))
    along(5, far, 1, (s, right)).wait_recv()
    start(across(3, far, 1))

    for place, owner in enumerate((b, left, right, far)):
        for half in (0, 1):
            for copy in across(place, owner, half):
                copy.wait_recv()
        for copy in image_across(place, owner, stamps_ref.at[3 * owner + 1]):
            copy.wait_recv()
    for copy in sends:
        copy.wait_send()
    for copy in own:
        copy.wait()

    def blank(side):
        for owner in range(n_batch):
            copy = pltpu.make_async_copy(zeros, window_ref.at[3 * owner + side], local_sem.at[0])
            other = pltpu.make_async_copy(zero_image, stamps_ref.at[3 * owner + side], local_sem.at[1])
            copy.start()
            other.start()
            copy.wait()
            other.wait()

    @pl.when(s == 0)
    def _():
        blank(0)

    @pl.when(s == n_sky - 1)
    def _():
        blank(2)


def gather_window(features, images, layer_mask):
    n_sky, n_batch = lax.axis_size("sky"), lax.axis_size("batch")
    return pl.pallas_call(
        functools.partial(gather_kernel, n_sky, n_batch),
        out_shape=(
            jax.ShapeDtypeStruct((CAND, NPIX, FEAT), F32),
            jax.ShapeDtypeStruct((CAND, LAYERS, TILE), F32),
        ),
        in_specs=[
            pl.BlockSpec(memory_space=pltpu.VMEM),
            pl.BlockSpec(memory_space=pltpu.VMEM),
            pl.BlockSpec(memory_space=pltpu.SMEM),
        ],
        out_specs=(pl.BlockSpec(memory_space=pl.ANY), pl.BlockSpec(memory_space=pl.ANY)),
        scratch_shapes=[
            pltpu.VMEM((LAYERS, TILE), F32),
            pltpu.VMEM((NPIX, FEAT), F32),
            pltpu.VMEM((LAYERS, TILE), F32),
            pltpu.SemaphoreType.DMA((2,)),
            pltpu.SemaphoreType.DMA((6,)),
            pltpu.SemaphoreType.DMA((6,)),
            pltpu.SemaphoreType.DMA((2, 8)),
            pltpu.SemaphoreType.DMA((2, 8)),
            pltpu.SemaphoreType.DMA((3,)),
            pltpu.SemaphoreType.DMA((3,)),
            pltpu.SemaphoreType.DMA((2, 4)),
            pltpu.SemaphoreType.DMA((2, 4)),
        ],
        compiler_params=pltpu.CompilerParams(collective_id=0, has_side_effects=True),
        name="gather_window",
    )(features, images, layer_mask)


def row_of(tile, index):
    return jnp.broadcast_to(tile[index : index + 1, :], (8, TILE))


def column_of(tile, index):
    return jnp.broadcast_to(tile[:, index : index + 1], (8, TILE))


def total(terms):
    while len(terms) > 1:
        terms = [terms[i] + terms[i + 1] if i + 1 < len(terms) else terms[i] for i in range(0, len(terms), 2)]
    return terms[0]


def invert_small(columns, row):
    columns = list(columns)
    for p in range(8):
        scale = 1.0 / row_of(columns[p], p)
        pivot = columns[p]
        here = row == p
        for j in range(8):
            if j != p:
                scaled = row_of(columns[j], p) * scale
                columns[j] = jnp.where(here, scaled, columns[j] - pivot * scaled)
        columns[p] = jnp.where(here, scale, -pivot * scale)
    return columns


def invert_tile(groups):
    row = lax.broadcasted_iota(jnp.int32, (8, TILE), 0)
    lane = lax.broadcasted_iota(jnp.int32, (8, TILE), 1)
    groups = list(groups)
    count = len(groups)
    for k in range(count):
        inside = (lane >= 8 * k) & (lane < 8 * k + 8)
        small = invert_small([column_of(groups[k], 8 * k + j) for j in range(8)], row)
        panel = jnp.where(inside, jnp.where(lane - 8 * k == row, 1.0, 0.0), groups[k])
        panel = total([small[j] * row_of(panel, j) for j in range(8)])
        rows = [row_of(panel, j) for j in range(8)]
        for step in range(1, count):
            i = (k + step) % count
            change = total([column_of(groups[i], 8 * k + j) * rows[j] for j in range(8)])
            groups[i] = jnp.where(inside, 0.0, groups[i]) - change
        groups[k] = panel
    return groups


def dot(a, b, dims=((1,), (0,))):
    return lax.dot_general(a, b, (dims, ((), ())), precision=HIGH, preferred_element_type=F32)


def halves(x):
    top = x.astype(BF16)
    return top, (x - top.astype(F32)).astype(BF16)


def solve_kernel(
    pair_ref, ridge_ref, window_ref, stamps_ref, target_ref, transfer_ref, coadd_ref,
    feats, images, target, system, right, left, inverse, sem,
):
    copies = []
    for k in range(NSEL):
        copies.append(
            pltpu.make_async_copy(window_ref.at[pair_ref[k]], feats.at[pl.ds(NPIX * k, NPIX)], sem.at[k])
        )
    fetch_target = pltpu.make_async_copy(target_ref, target, sem.at[NSEL])
    for copy in copies:
        copy.start()
    fetch_target.start()
    fetch_images = []
    for k in range(NSEL):
        fetch_images.append(pltpu.make_async_copy(stamps_ref.at[pair_ref[k]], images.at[k], sem.at[NSEL + 1 + k]))
        fetch_images[k].start()
    feats[ORDER:, :] = jnp.zeros((PADDED - ORDER, FEAT), F32)
    for copy in copies:
        copy.wait()

    system[...] = dot(feats[...], feats[...], ((1,), (1,)))
    ridge = ridge_ref[0]
    eye = jnp.where(
        lax.broadcasted_iota(jnp.int32, (TILE, TILE), 0) == lax.broadcasted_iota(jnp.int32, (TILE, TILE), 1),
        ridge, 0.0,
    )
    for k in range(NBLOCK):
        at = pl.ds(TILE * k, TILE)
        system[at, at] += eye
    fetch_target.wait()
    right[...] = dot(feats[...], target[...], ((1,), (1,)))

    def eliminate(k, carry):
        at = pl.ds(pl.multiple_of(TILE * k, TILE), TILE)
        groups = [
            system[pl.ds(pl.multiple_of(TILE * k + 8 * i, 8), 8), at] for i in range(TILE // 8)
        ]
        groups = invert_tile(groups)
        for i in range(TILE // 8):
            inverse[8 * i : 8 * i + 8, :] = groups[i]
        left[...] = dot(system[:, at], inverse[...])
        left[at, :] = -inverse[...]
        across = system[at, :]
        system[at, :] = jnp.zeros((TILE, PADDED), F32)
        left_top, left_low = halves(left[...])
        across_top, across_low = halves(across)
        change = jnp.dot(
            jnp.concatenate([left_top, left_low], axis=1),
            jnp.concatenate([across_top, across_top], axis=0),
            preferred_element_type=F32,
        )
        change += jnp.dot(left_top, across_low, preferred_element_type=F32)
        system[...] -= change
        system[:, at] = -left[...]
        return carry

    lax.fori_loop(0, NBLOCK, eliminate, 0)
    transfer = dot(system[:ORDER, :], right[...])
    transfer_ref[...] = transfer
    result = jnp.zeros((LAYERS, NOUT_PIX), F32)
    for k in range(NSEL):
        fetch_images[k].wait()
        result += dot(images[k][:, :NPIX], transfer_ref[NPIX * k : NPIX * k + NPIX, :])
    coadd_ref[...] = result


def solve(pair_list, ridge, window, stamps, target):
    return pl.pallas_call(
        solve_kernel,
        out_shape=(
            jax.ShapeDtypeStruct((ORDER, NOUT_PIX), F32),
            jax.ShapeDtypeStruct((LAYERS, NOUT_PIX), F32),
        ),
        in_specs=[
            pl.BlockSpec(memory_space=pltpu.SMEM),
            pl.BlockSpec(memory_space=pltpu.SMEM),
            pl.BlockSpec(memory_space=pl.ANY),
            pl.BlockSpec(memory_space=pl.ANY),
            pl.BlockSpec(memory_space=pl.ANY),
        ],
        out_specs=(pl.BlockSpec(memory_space=pltpu.VMEM), pl.BlockSpec(memory_space=pltpu.VMEM)),
        scratch_shapes=[
            pltpu.VMEM((PADDED, FEAT), F32),
            pltpu.VMEM((NSEL, LAYERS, TILE), F32),
            pltpu.VMEM((NOUT_PIX, FEAT), F32),
            pltpu.VMEM((PADDED, PADDED), F32),
            pltpu.VMEM((PADDED, NOUT_PIX), F32),
            pltpu.VMEM((PADDED, TILE), F32),
            pltpu.VMEM((TILE, TILE), F32),
            pltpu.SemaphoreType.DMA((2 * NSEL + 1,)),
        ],
        compiler_params=pltpu.CompilerParams(vmem_limit_bytes=48 << 20),
        name="solve_stamp",
    )(pair_list, ridge, window, stamps, target)


def blend_kernel(n_sky, n_batch, coadd_ref, out_ref, slots, send_sem, recv_sem):
    s = lax.axis_index("sky")
    b = lax.axis_index("batch")
    up = lax.rem(s + 1, n_sky)
    down = lax.rem(s + n_sky - 1, n_sky)
    right = lax.rem(b + 1, n_batch)
    left = lax.rem(b + n_batch - 1, n_batch)
    where = ((down, b), (up, b), (s, left), (s, right))
    barrier = pltpu.get_barrier_semaphore()
    for device in where:
        pl.semaphore_signal(barrier, inc=1, device_id=device, device_id_type=MESH)
    pl.semaphore_wait(barrier, 4)
    copies = [
        pltpu.make_async_remote_copy(
            src_ref=coadd_ref, dst_ref=slots.at[n], send_sem=send_sem.at[n], recv_sem=recv_sem.at[n],
            device_id=where[n], device_id_type=MESH,
        )
        for n in range(4)
    ]
    for copy in copies:
        copy.start()
    pixel = lax.broadcasted_iota(jnp.int32, (1, NOUT_PIX), 1)
    line = pixel // SIDE
    place = pixel - line * SIDE
    edge = SIDE - FADE

    def weight(at, low, first, step, there):
        value = (first + step * (at - low)).astype(F32) / (FADE + 1.0)
        value = jnp.where((at >= low) & (at < low + FADE), value, 0.0)
        return jnp.where(there, value, 0.0)

    weights = (
        weight(place, edge, 1, 1, s < n_sky - 1),
        weight(place, 0, FADE, -1, s > 0),
        weight(line, edge, 1, 1, b < n_batch - 1),
        weight(line, 0, FADE, -1, b > 0),
    )
    shifts = (edge, -edge, edge * SIDE, -edge * SIDE)
    result = coadd_ref[...]
    for n in range(4):
        copies[n].wait_recv()
        other = slots[n]
        shift = shifts[n] % NOUT_PIX
        moved = jnp.concatenate([other[:, NOUT_PIX - shift :], other[:, : NOUT_PIX - shift]], axis=1)
        result = result + weights[n] * moved
    out_ref[...] = result
    for copy in copies:
        copy.wait_send()


def blend(coadd):
    n_sky, n_batch = lax.axis_size("sky"), lax.axis_size("batch")
    return pl.pallas_call(
        functools.partial(blend_kernel, n_sky, n_batch),
        out_shape=jax.ShapeDtypeStruct((LAYERS, NOUT_PIX), F32),
        in_specs=[pl.BlockSpec(memory_space=pltpu.VMEM)],
        out_specs=pl.BlockSpec(memory_space=pltpu.VMEM),
        scratch_shapes=[
            pltpu.VMEM((4, LAYERS, NOUT_PIX), F32),
            pltpu.SemaphoreType.DMA((4,)),
            pltpu.SemaphoreType.DMA((4,)),
        ],
        compiler_params=pltpu.CompilerParams(collective_id=1, has_side_effects=True),
        name="blend_edges",
    )(coadd)


def local(features, target, images, layer_mask, pair_list, ridge_weight):
    window, stamps = gather_window(
        features.reshape(NPIX, FEAT), images.reshape(LAYERS, NPIX), layer_mask.reshape(LAYERS)
    )
    transfer, coadd = solve(
        pair_list.reshape(NSEL), ridge_weight.reshape(1), window, stamps, target.reshape(NOUT_PIX, FEAT)
    )
    final = blend(coadd)
    return (transfer.reshape(1, 1, ORDER, NOUT_PIX), final.reshape(LAYERS, SIDE, SIDE))


def solution(mesh):
    in_specs = (
        P("batch", "sky", None, None),
        P("batch", "sky", None, None),
        P("batch", "sky", None, None),
        P("batch", "sky", None),
        P("batch", "sky", None),
        P("batch", "sky"),
    )
    out_specs = (P("batch", "sky", None, None), P(None, "batch", "sky"))
    return jax.shard_map(local, mesh=mesh, in_specs=in_specs, out_specs=out_specs, check_vma=False)
```

profile of v0, /device:TPU:6, one launch (start us, length us, event | category | flops | bytes accessed | tf_op | source)
XLA Modules:
  0.0 99.4 jit_solution(16777536219571270790)
XLA Ops:
  1.3 31.3 %gather_window.1 = (f32[12,80,1024]{2,1,0:T(8,128)}, f32[12,16,128]{2,1,0:T(8,128)}) custom-call(f32[80,1024]{1,0:T(8,128)} %bitcast.11, f32[16,80]{1,0:T(8,128)} %bitcast.12, s32[16]{0:T(128)} %bitcast.13), custom_call_target="tpu_custom_call" | custom-call | tf_op jit(solution)/shard_map/gather_window/pallas_call | solution.py:168
  32.6 0.0 copy-start
  32.6 1.7 %copy-done = f32[1,1,576,1024]{3,2,1,0:T(8,128)S(1)} copy-done((f32[1,1,576,1024]{3,2,1,0:T(8,128)S(1)}, f32[1,1,576,1024]{3,2,1,0:T(8,128)}, u32[]{:S(2)}) %copy-start) | copy-done | bytes 2359320
  34.2 0.0 copy-start.1
  34.2 0.9 copy-done.1
  35.1 0.0 copy-start.3
  35.1 0.7 copy-done.3
  35.8 50.7 %solve_stamp.1 = (f32[720,576]{1,0:T(8,128)S(1)}, f32[16,576]{1,0:T(8,128)S(1)}) custom-call(s32[9]{0:T(128)S(1)} %bitcast.10, f32[1]{0:T(128)} %bitcast.7.ridge_ref, f32[12,80,1024]{2,1,0:T(8,128)} %get-tuple-element.6.window_ref, f32[12,16,128]{2,1,0:T(8,128)S(1)} %copy-done.1, f32[576,1024]{1,0:T(8,128)S(1)} %bitcast.8), custom_call_target="tpu_custom_call" | custom-call | tf_op jit(solution)/shard_map/solve_stamp/pallas_call | solution.py:323
  86.5 0.0 copy-start.2
  86.5 0.6 copy-done.2
  87.1 1.8 %copy.8 = f32[1,1,720,576]{2,3,1,0:T(8,128)} copy(f32[1,1,720,576]{3,2,1,0:T(8,128)S(1)} %bitcast.9) | data formatting | bytes 3317760
  88.9 8.9 %blend_edges.1 = f32[16,576]{1,0:T(8,128)} custom-call(f32[16,576]{1,0:T(8,128)} %copy-done.2), custom_call_target="tpu_custom_call" | custom-call | tf_op jit(solution)/shard_map/blend_edges/pallas_call | solution.py:404
  97.8 1.6 %reshape.35 = f32[16,24,24]{2,1,0:T(8,128)} reshape(f32[16,576]{1,0:T(8,128)} %blend_edges.1) | data formatting | bytes 73728 | tf_op jit(solution)/shard_map/reshape | solution.py:427
Async XLA Ops:
  32.6 1.7 %copy-start = (f32[1,1,576,1024]{3,2,1,0:T(8,128)S(1)}, f32[1,1,576,1024]{3,2,1,0:T(8,128)}, u32[]{:S(2)}) copy-start(f32[1,1,576,1024]{3,2,1,0:T(8,128)} %param.7) | copy-start | bytes 7077892
  34.2 0.9 copy-start.1
  35.1 0.7 copy-start.3
  86.5 0.6 copy-start.2
where the time goes:
time: 99.8 us; the launch traced here: 99.4 us
  Pallas kernels  90.9 us (91%)
  local copies, waits for them, and re-layouts  7.16 us (7%)
  between operations  1.32 us (1%)
    pallas_call x1, Pallas kernels, solve(): pl.pallas_call(solve_kernel, out_shape=(jax.ShapeDtypeStruct((ORDER, NOUT...  50.7 us
    pallas_call x1, Pallas kernels, gather_window(): pl.pallas_call(functools.partial(gather_kernel, n_sky, n_batch), out_shap...  31.3 us
    pallas_call x1, Pallas kernels, blend(): pl.pallas_call(functools.partial(blend_kernel, n_sky, n_batch), out_shape...  8.93 us
    unnamed x9, local copies, waits for them, and re-layouts  5.58 us

commit v1 on v0

--- a/solution.py
+++ b/solution.py
@@ -23,6 +23,7 @@
 HALF = NPIX // 2
 MESH = pl.DeviceIdType.MESH
 HIGH = lax.Precision.HIGH
+NT = (((1,), (1,)), ((), ()))
 F32 = jnp.float32
 BF16 = jnp.bfloat16
 
@@ -210,36 +211,92 @@
     return terms[0]
 
 
-def invert_small(columns, row):
-    columns = list(columns)
+def reduce_single(block, carried, row):
+    block, carried = list(block), list(carried)
     for p in range(8):
-        scale = 1.0 / row_of(columns[p], p)
-        pivot = columns[p]
+        scale = 1.0 / row_of(block[p], p)
+        pivot = block[p]
         here = row == p
-        for j in range(8):
-            if j != p:
-                scaled = row_of(columns[j], p) * scale
-                columns[j] = jnp.where(here, scaled, columns[j] - pivot * scaled)
-        columns[p] = jnp.where(here, scale, -pivot * scale)
-    return columns
-
-
-def invert_tile(groups):
+
+        def step(tile):
+            scaled = row_of(tile, p) * scale
+            return jnp.where(here, scaled, tile - pivot * scaled)
+
+        for j in range(p + 1, 8):
+            block[j] = step(block[j])
+        carried = [step(tile) for tile in carried]
+    return carried
+
+
+def reduce_paired(block, carried, row):
+    block, carried = list(block), list(carried)
+    for p in range(0, 8, 2):
+        q = p + 1
+        first, mixed, second = row_of(block[p], p), row_of(block[q], p), row_of(block[q], q)
+        scale = 1.0 / (first * second - mixed * mixed)
+        upper, cross, lower = second * scale, mixed * scale, first * scale
+        pivot_p, pivot_q = block[p], block[q]
+        at_p, at_q = row == p, row == q
+
+        def step(tile):
+            x, y = row_of(tile, p), row_of(tile, q)
+            new_p = upper * x - cross * y
+            new_q = lower * y - cross * x
+            return jnp.where(at_p, new_p, jnp.where(at_q, new_q, tile - (pivot_p * new_p + pivot_q * new_q)))
+
+        for j in range(q + 1, 8):
+            block[j] = step(block[j])
+        carried = [step(tile) for tile in carried]
+    return carried
+
+
+def invert_tile(groups, jobs):
     row = lax.broadcasted_iota(jnp.int32, (8, TILE), 0)
     lane = lax.broadcasted_iota(jnp.int32, (8, TILE), 1)
     groups = list(groups)
     count = len(groups)
-    for k in range(count):
-        inside = (lane >= 8 * k) & (lane < 8 * k + 8)
-        small = invert_small([column_of(groups[k], 8 * k + j) for j in range(8)], row)
-        panel = jnp.where(inside, jnp.where(lane - 8 * k == row, 1.0, 0.0), groups[k])
-        panel = total([small[j] * row_of(panel, j) for j in range(8)])
-        rows = [row_of(panel, j) for j in range(8)]
-        for step in range(1, count):
-            i = (k + step) % count
-            change = total([column_of(groups[i], 8 * k + j) * rows[j] for j in range(8)])
-            groups[i] = jnp.where(inside, 0.0, groups[i]) - change
-        groups[k] = panel
+    zero = jnp.zeros((16, TILE), BF16)
+    for k0 in range(0, count, 2):
+        k1 = k0 + 1
+        in0 = (lane >= 8 * k0) & (lane < 8 * k0 + 8)
+        in1 = (lane >= 8 * k1) & (lane < 8 * k1 + 8)
+        inside = in0 | in1
+        top, low = groups[k0], groups[k1]
+        near = [k1 + 1, k1 + 2] if k1 + 2 < count else []
+        far = [i for i in range(count) if i not in near and i not in (k0, k1)]
+        diag = [column_of(top, 8 * k0 + j) for j in range(8)]
+        beside = [column_of(top, 8 * k1 + j) for j in range(8)]
+        below = [column_of(low, 8 * k0 + j) for j in range(8)]
+        corner = [column_of(low, 8 * k1 + j) for j in range(8)]
+        factors = {i: [column_of(groups[i], 8 * k0 + j) for j in range(16)] for i in near}
+        for job in jobs[k0 // 2 * len(jobs) * 2 // count : (k0 // 2 + 1) * len(jobs) * 2 // count]:
+            job()
+        panel = jnp.where(in0, jnp.where(lane - 8 * k0 == row, 1.0, 0.0), top)
+        out = reduce_single(diag, beside + [panel], row)
+        upper, top = out[:8], out[8]
+        corner = [corner[m] - total([below[j] * row_of(upper[m], j) for j in range(8)]) for m in range(8)]
+        low = jnp.where(in0, 0.0, low) - total([below[j] * row_of(top, j) for j in range(8)])
+        panel = jnp.where(in1, jnp.where(lane - 8 * k1 == row, 1.0, 0.0), low)
+        low = reduce_paired(corner, [panel], row)[0]
+        low_rows = [row_of(low, j) for j in range(8)]
+        top = jnp.where(in1, 0.0, top) - total([upper[j] * low_rows[j] for j in range(8)])
+        rows = [row_of(top, j) for j in range(8)] + low_rows
+        groups[k0], groups[k1] = top, low
+        old = jnp.concatenate([groups[i] for i in far], axis=0)
+        for i in near:
+            groups[i] = jnp.where(inside, 0.0, groups[i]) - total([factors[i][j] * rows[j] for j in range(16)])
+        old_top, old_low = halves(old)
+        new_top, new_low = halves(jnp.concatenate([top, low], axis=0))
+        before, after = [zero] * (k0 // 2), [zero] * (TILE // 16 - 1 - k0 // 2)
+        new_top = jnp.concatenate(before + [new_top] + after, axis=0)
+        new_low = jnp.concatenate(before + [new_low] + after, axis=0)
+        change = jnp.dot(
+            jnp.concatenate([old_top, old_low], axis=1),
+            jnp.concatenate([new_top, new_top], axis=0),
+            preferred_element_type=F32,
+        ) + jnp.dot(old_top, new_low, preferred_element_type=F32)
+        for n, i in enumerate(far):
+            groups[i] = jnp.where(inside, 0.0, groups[i]) - change[8 * n : 8 * n + 8]
     return groups
 
 
@@ -254,7 +311,8 @@
 
 def solve_kernel(
     pair_ref, ridge_ref, window_ref, stamps_ref, target_ref, transfer_ref, coadd_ref,
-    feats, images, target, system, right, left, inverse, sem,
+    feats, images, target, feat_top, feat_low, target_top, target_low, system, right,
+    left_top, left_low, across_top, across_low, diag, inverse, previous, sem,
 ):
     copies = []
     for k in range(NSEL):
@@ -264,16 +322,31 @@
     fetch_target = pltpu.make_async_copy(target_ref, target, sem.at[NSEL])
     for copy in copies:
         copy.start()
-    fetch_target.start()
     fetch_images = []
     for k in range(NSEL):
         fetch_images.append(pltpu.make_async_copy(stamps_ref.at[pair_ref[k]], images.at[k], sem.at[NSEL + 1 + k]))
         fetch_images[k].start()
-    feats[ORDER:, :] = jnp.zeros((PADDED - ORDER, FEAT), F32)
-    for copy in copies:
-        copy.wait()
-
-    system[...] = dot(feats[...], feats[...], ((1,), (1,)))
+    fetch_target.start()
+    feat_top[ORDER:, :] = jnp.zeros((PADDED - ORDER, FEAT), BF16)
+    feat_low[ORDER:, :] = jnp.zeros((PADDED - ORDER, FEAT), BF16)
+    for k in range(NSEL):
+        copies[k].wait()
+        rows = pl.ds(NPIX * k, NPIX)
+        feat_top[rows, :], feat_low[rows, :] = halves(feats[rows, :])
+
+    def product(a_top, a_low, b_top, b_low):
+        result = lax.dot_general(a_top, b_top, NT, preferred_element_type=F32)
+        result += lax.dot_general(a_top, b_low, NT, preferred_element_type=F32)
+        return result + lax.dot_general(a_low, b_top, NT, preferred_element_type=F32)
+
+    wide = 2 * TILE
+    for k in range(PADDED // wide):
+        rows, rest = pl.ds(wide * k, wide), pl.ds(wide * k, PADDED - wide * k)
+        system[rows, rest] = product(feat_top[rows, :], feat_low[rows, :], feat_top[rest, :], feat_low[rest, :])
+    for k in range(PADDED // wide):
+        for j in range(k):
+            rows, columns = pl.ds(wide * k, wide), pl.ds(wide * j, wide)
+            system[rows, columns] = system[columns, rows].T
     ridge = ridge_ref[0]
     eye = jnp.where(
         lax.broadcasted_iota(jnp.int32, (TILE, TILE), 0) == lax.broadcasted_iota(jnp.int32, (TILE, TILE), 1),
@@ -282,69 +355,141 @@
     for k in range(NBLOCK):
         at = pl.ds(TILE * k, TILE)
         system[at, at] += eye
+    diag[...] = system[:TILE, :TILE]
     fetch_target.wait()
-    right[...] = dot(feats[...], target[...], ((1,), (1,)))
+    for copy in fetch_images:
+        copy.wait()
+
+    third = PADDED // 3
+
+    def left_job(j, part):
+        def job():
+            at = pl.ds(pl.multiple_of(TILE * j, TILE), TILE)
+            rows = pl.ds(third * part, third)
+            left = dot(system[rows, at], previous[...])
+            system[rows, at] = -left
+            left_top[rows, :], left_low[rows, :] = halves(left)
+        return job
+
+    def across_job(j):
+        def job():
+            at = pl.ds(pl.multiple_of(TILE * j, TILE), TILE)
+            across_top[...], across_low[...] = halves(system[at, :])
+            system[at, :] = jnp.zeros((TILE, PADDED), F32)
+            system[at, at] = previous[...]
+            top, low = halves(-previous[...])
+            left_top[at, :] = top
+            left_low[at, :] = low
+            across_top[:, at] = jnp.zeros((TILE, TILE), BF16)
+            across_low[:, at] = jnp.zeros((TILE, TILE), BF16)
+        return job
+
+    def update_job(part):
+        def job():
+            columns = pl.ds(third * part, third)
+            top = across_top[:, columns]
+            change = jnp.dot(
+                jnp.concatenate([left_top[...], left_low[...]], axis=1),
+                jnp.concatenate([top, top], axis=0),
+                preferred_element_type=F32,
+            )
+            change += jnp.dot(left_top[...], across_low[:, columns], preferred_element_type=F32)
+            system[:, columns] -= change
+        return job
+
+    def split_job(part):
+        def job():
+            rows = pl.ds(NOUT_PIX // 3 * part, NOUT_PIX // 3)
+            target_top[rows, :], target_low[rows, :] = halves(target[rows, :])
+        return job
+
+    def right_job(j, part):
+        def job():
+            at = pl.ds(pl.multiple_of(TILE * j, TILE), TILE)
+            share = NOUT_PIX // 3
+            rows = pl.ds(share * part, share)
+            right[rows, at] = product(target_top[rows, :], target_low[rows, :], feat_top[at, :], feat_low[at, :])
+        return job
+
+    def invert(rows, jobs):
+        groups = invert_tile([diag[8 * i : 8 * i + 8, :] for i in range(rows // 8)], jobs)
+        for i, group in enumerate(groups):
+            inverse[8 * i : 8 * i + 8, :] = group
+
+    def advance(k):
+        at = pl.ds(pl.multiple_of(TILE * k, TILE), TILE)
+        then = pl.ds(pl.multiple_of(TILE * k + TILE, TILE), TILE)
+        diag[...] = system[then, then] - dot(dot(system[then, at], inverse[...]), system[at, then])
+        previous[...] = inverse[...]
+
+    def jobs_after(j):
+        return [left_job(j, part) for part in range(3)] + [across_job(j)] + [update_job(part) for part in range(3)]
+
+    invert(TILE, [split_job(part) for part in range(3)] + [right_job(0, part) for part in range(3)])
+    advance(0)
 
     def eliminate(k, carry):
-        at = pl.ds(pl.multiple_of(TILE * k, TILE), TILE)
-        groups = [
-            system[pl.ds(pl.multiple_of(TILE * k + 8 * i, 8), 8), at] for i in range(TILE // 8)
-        ]
-        groups = invert_tile(groups)
-        for i in range(TILE // 8):
-            inverse[8 * i : 8 * i + 8, :] = groups[i]
-        left[...] = dot(system[:, at], inverse[...])
-        left[at, :] = -inverse[...]
-        across = system[at, :]
-        system[at, :] = jnp.zeros((TILE, PADDED), F32)
-        left_top, left_low = halves(left[...])
-        across_top, across_low = halves(across)
-        change = jnp.dot(
-            jnp.concatenate([left_top, left_low], axis=1),
-            jnp.concatenate([across_top, across_top], axis=0),
-            preferred_element_type=F32,
-        )
-        change += jnp.dot(left_top, across_low, preferred_element_type=F32)
-        system[...] -= change
-        system[:, at] = -left[...]
+        invert(TILE, jobs_after(k - 1) + [right_job(k, part) for part in range(3)])
+        advance(k)
         return carry
 
-    lax.fori_loop(0, NBLOCK, eliminate, 0)
-    transfer = dot(system[:ORDER, :], right[...])
-    transfer_ref[...] = transfer
-    result = jnp.zeros((LAYERS, NOUT_PIX), F32)
+    lax.fori_loop(1, NBLOCK - 1, eliminate, 0)
+    last = NBLOCK - 1
+    inverse[...] = jnp.zeros((TILE, TILE), F32)
+    invert(ORDER - TILE * last, jobs_after(last - 1) + [right_job(last, part) for part in range(3)])
+    previous[...] = inverse[...]
+    for job in jobs_after(last):
+        job()
+    transfer = dot(right[...], system[...])
+    transfer_ref[...] = transfer[:, :ORDER]
+
+    empty = jnp.zeros((LAYERS, TILE), F32)
+    strips = [empty] * (NBLOCK + 1)
     for k in range(NSEL):
-        fetch_images[k].wait()
-        result += dot(images[k][:, :NPIX], transfer_ref[NPIX * k : NPIX * k + NPIX, :])
-    coadd_ref[...] = result
+        first, shift = divmod(NPIX * k, TILE)
+        wide = jnp.concatenate([images[k], empty], axis=1)
+        if shift:
+            wide = pltpu.roll(wide, shift, 1)
+        strips[first] = strips[first] + wide[:, :TILE]
+        strips[first + 1] = strips[first + 1] + wide[:, TILE:]
+    coadd_ref[...] = dot(jnp.concatenate(strips[:NBLOCK], axis=1), transfer, ((1,), (1,)))
 
 
 def solve(pair_list, ridge, window, stamps, target):
     return pl.pallas_call(
         solve_kernel,
         out_shape=(
-            jax.ShapeDtypeStruct((ORDER, NOUT_PIX), F32),
+            jax.ShapeDtypeStruct((NOUT_PIX, ORDER), F32),
             jax.ShapeDtypeStruct((LAYERS, NOUT_PIX), F32),
         ),
         in_specs=[
             pl.BlockSpec(memory_space=pltpu.SMEM),
             pl.BlockSpec(memory_space=pltpu.SMEM),
-            pl.BlockSpec(memory_space=pl.ANY),
-            pl.BlockSpec(memory_space=pl.ANY),
-            pl.BlockSpec(memory_space=pl.ANY),
+            pl.BlockSpec(memory_space=pltpu.HBM),
+            pl.BlockSpec(memory_space=pltpu.HBM),
+            pl.BlockSpec(memory_space=pltpu.HBM),
         ],
         out_specs=(pl.BlockSpec(memory_space=pltpu.VMEM), pl.BlockSpec(memory_space=pltpu.VMEM)),
         scratch_shapes=[
             pltpu.VMEM((PADDED, FEAT), F32),
             pltpu.VMEM((NSEL, LAYERS, TILE), F32),
             pltpu.VMEM((NOUT_PIX, FEAT), F32),
+            pltpu.VMEM((PADDED, FEAT), BF16),
+            pltpu.VMEM((PADDED, FEAT), BF16),
+            pltpu.VMEM((NOUT_PIX, FEAT), BF16),
+            pltpu.VMEM((NOUT_PIX, FEAT), BF16),
             pltpu.VMEM((PADDED, PADDED), F32),
-            pltpu.VMEM((PADDED, NOUT_PIX), F32),
-            pltpu.VMEM((PADDED, TILE), F32),
+            pltpu.VMEM((NOUT_PIX, PADDED), F32),
+            pltpu.VMEM((PADDED, TILE), BF16),
+            pltpu.VMEM((PADDED, TILE), BF16),
+            pltpu.VMEM((TILE, PADDED), BF16),
+            pltpu.VMEM((TILE, PADDED), BF16),
+            pltpu.VMEM((TILE, TILE), F32),
+            pltpu.VMEM((TILE, TILE), F32),
             pltpu.VMEM((TILE, TILE), F32),
             pltpu.SemaphoreType.DMA((2 * NSEL + 1,)),
         ],
-        compiler_params=pltpu.CompilerParams(vmem_limit_bytes=48 << 20),
+        compiler_params=pltpu.CompilerParams(vmem_limit_bytes=56 << 20),
         name="solve_stamp",
     )(pair_list, ridge, window, stamps, target)
 
@@ -424,7 +569,7 @@
         pair_list.reshape(NSEL), ridge_weight.reshape(1), window, stamps, target.reshape(NOUT_PIX, FEAT)
     )
     final = blend(coadd)
-    return (transfer.reshape(1, 1, ORDER, NOUT_PIX), final.reshape(LAYERS, SIDE, SIDE))
+    return (transfer.T.reshape(1, 1, ORDER, NOUT_PIX), final.reshape(LAYERS, SIDE, SIDE))
 
 
 def solution(mesh):

time: 99.8 us -> 74.8 us (0.75)
  Pallas kernels: 90.9 us -> 71.7 us
  local copies, waits for them, and re-layouts: 7.16 us -> 1.58 us
    pallas_call x1, Pallas kernels: 50.7 us -> 31.4 us  [solve(): pl.pallas_call(solve_kernel, out_shape=(jax.ShapeDtypeStruct((NOUT_PIX, O...]
    unnamed x9 -> x0, local copies, waits for them, and re-layouts: 5.58 us -> none
where the time goes in v1:
time: 74.8 us; the launch traced here: 74.6 us
  Pallas kernels  71.7 us (96%)
  local copies, waits for them, and re-layouts  1.58 us (2%)
  between operations  1.3 us (2%)
    pallas_call x1, Pallas kernels, solve(): pl.pallas_call(solve_kernel, out_shape=(jax.ShapeDtypeStruct((NOUT_PIX, O...  31.4 us
    pallas_call x1, Pallas kernels, gather_window(): pl.pallas_call(functools.partial(gather_kernel, n_sky, n_batch), out_shap...  31.3 us
    pallas_call x1, Pallas kernels, blend(): pl.pallas_call(functools.partial(blend_kernel, n_sky, n_batch), out_shape...  9.06 us
    reshape x1, local copies, waits for them, and re-layouts, local(): final.reshape(LAYERS, SIDE, SIDE)  1.58 us

profile of v1, /device:TPU:6, one launch (start us, length us, event | category | flops | bytes accessed | tf_op | source)
XLA Modules:
  0.0 74.6 jit_solution(14367948924050111402)
XLA Ops:
  1.3 31.3 %gather_window.1 = (f32[12,80,1024]{2,1,0:T(8,128)}, f32[12,16,128]{2,1,0:T(8,128)}) custom-call(f32[80,1024]{1,0:T(8,128)} %bitcast.11, f32[16,80]{1,0:T(8,128)} %bitcast.12, s32[16]{0:T(128)} %bitcast.13), custom_call_target="tpu_custom_call" | custom-call | tf_op jit(solution)/shard_map/gather_window/pallas_call | solution.py:169
  32.6 31.4 %solve_stamp.1 = (f32[576,720]{1,0:T(8,128)}, f32[16,576]{1,0:T(8,128)}) custom-call(s32[9]{0:T(128)} %bitcast.14, f32[1]{0:T(128)} %bitcast.9.ridge_ref, f32[12,80,1024]{2,1,0:T(8,128)} %get-tuple-element.6.window_ref, f32[12,16,128]{2,1,0:T(8,128)} %get-tuple-element.7.stamps_ref, f32[576,1024]{1,0:T(8,128)} %bitcast.10), custom_call_target="tpu_custom_call" | custom-call | tf_op jit(solution)/shard_map/solve_stamp/pallas_call | solution.py:459
  63.9 9.1 %blend_edges.1 = f32[16,576]{1,0:T(8,128)} custom-call(f32[16,576]{1,0:T(8,128)} %get-tuple-element.9.coadd_ref), custom_call_target="tpu_custom_call" | custom-call | tf_op jit(solution)/shard_map/blend_edges/pallas_call | solution.py:549
  73.0 1.6 %reshape.35 = f32[16,24,24]{2,1,0:T(8,128)} reshape(f32[16,576]{1,0:T(8,128)} %blend_edges.1) | data formatting | bytes 73728 | tf_op jit(solution)/shard_map/reshape | solution.py:572

commit v2 on v1

--- a/solution.py
+++ b/solution.py
@@ -20,7 +20,7 @@
 TILE = 128
 NBLOCK = 6
 PADDED = TILE * NBLOCK
-HALF = NPIX // 2
+PARTS = (pl.ds(0, 24), pl.ds(24, 16), pl.ds(40, 24), pl.ds(64, 16))
 MESH = pl.DeviceIdType.MESH
 HIGH = lax.Precision.HIGH
 NT = (((1,), (1,)), ((), ()))
@@ -28,9 +28,14 @@
 BF16 = jnp.bfloat16
 
 
+def halves(x):
+    top = x.astype(BF16)
+    return top, (x - top.astype(F32)).astype(BF16)
+
+
 def gather_kernel(
-    n_sky, n_batch, feat_ref, image_ref, mask_ref, window_ref, stamps_ref,
-    masked, zeros, zero_image, local_sem, fs_sem, fr_sem, ys_sem, yr_sem, is_sem, ir_sem, js_sem, jr_sem,
+    n_sky, n_batch, feat_ref, image_ref, mask_ref, target_ref, top_ref, low_ref, stamps_ref, target_top_ref, target_low_ref,
+    window, target, masked, top, low, target_top, target_low, local_sem, out_sem, fs_sem, fr_sem, ys_sem, yr_sem, is_sem, ir_sem, js_sem, jr_sem,
 ):
     s = lax.axis_index("sky")
     b = lax.axis_index("batch")
@@ -43,6 +48,10 @@
     barrier = pltpu.get_barrier_semaphore()
     for where in ((s, left), (s, right), (up, b), (down, b)):
         pl.semaphore_signal(barrier, inc=1, device_id=where, device_id_type=MESH)
+    fetch_target = pltpu.make_async_copy(target_ref, target, local_sem.at[0])
+    fetch_target.start()
+    fetch_own = pltpu.make_async_copy(feat_ref, window.at[3 * b + 1], local_sem.at[1])
+    fetch_own.start()
 
     row = lax.broadcasted_iota(jnp.int32, (LAYERS, NPIX), 0)
     keep = jnp.zeros((LAYERS, NPIX), jnp.int32)
@@ -50,54 +59,28 @@
         keep = jnp.where(row == layer, mask_ref[layer], keep)
     masked[...] = jnp.zeros((LAYERS, TILE), F32)
     masked[:, :NPIX] = image_ref[...] * keep.astype(F32)
-    zeros[...] = jnp.zeros((NPIX, FEAT), F32)
-    zero_image[...] = jnp.zeros((LAYERS, TILE), F32)
 
     pl.semaphore_wait(barrier, 4)
-
-    rows = (pl.ds(0, HALF), pl.ds(HALF, HALF))
 
     def remote(src, dst, send, recv, where):
         return pltpu.make_async_remote_copy(
             src_ref=src, dst_ref=dst, send_sem=send, recv_sem=recv, device_id=where, device_id_type=MESH
         )
 
-    def along(number, owner, half, where, src=None):
-        slot = window_ref.at[3 * owner + 1, rows[half]]
-        return remote(slot if src is None else src, slot, fs_sem.at[number], fr_sem.at[number], where)
-
-    own_half = (feat_ref.at[rows[0]], feat_ref.at[rows[1]])
-    sends = []
-    for half in (0, 1):
-        sends += [
-            along(0 + half, b, half, (s, right), own_half[half]),
-            along(2 + half, b, half, (s, left), own_half[half]),
-        ]
-        for copy in sends[-2:]:
-            copy.start()
-
-    def across(place, owner, half, src=None):
-        base = window_ref.at[3 * owner + 1, rows[half]] if src is None else src
-        number = 2 * place + half
+    def along(direction, number, owner, part, src=None):
+        slot = window.at[3 * owner + 1, PARTS[part]]
+        where = (s, left) if direction else (s, right)
+        return remote(
+            slot if src is None else src, slot, fs_sem.at[direction, number], fr_sem.at[direction, number], where
+        )
+
+    def across(place, owner, part, src=None):
+        base = window.at[3 * owner + 1, PARTS[part]] if src is None else src
+        number = 4 * place + part
         return (
-            remote(base, window_ref.at[3 * owner, rows[half]], ys_sem.at[0, number], yr_sem.at[0, number], (up, b)),
-            remote(base, window_ref.at[3 * owner + 2, rows[half]], ys_sem.at[1, number], yr_sem.at[1, number], (down, b)),
+            remote(base, window.at[3 * owner, PARTS[part]], ys_sem.at[0, number], yr_sem.at[0, number], (up, b)),
+            remote(base, window.at[3 * owner + 2, PARTS[part]], ys_sem.at[1, number], yr_sem.at[1, number], (down, b)),
         )
-
-    def start(copies):
-        for copy in copies:
-            copy.start()
-        sends.extend(copies)
-
-    for half in (0, 1):
-        start(across(0, b, half, own_half[half]))
-
-    own = [
-        pltpu.make_async_copy(feat_ref, window_ref.at[3 * b + 1], local_sem.at[0]),
-        pltpu.make_async_copy(masked, stamps_ref.at[3 * b + 1], local_sem.at[1]),
-    ]
-    for copy in own:
-        copy.start()
 
     def image_along(number, owner, where, src):
         return remote(src, stamps_ref.at[3 * owner + 1], is_sem.at[number], ir_sem.at[number], where)
@@ -108,93 +91,138 @@
             remote(src, stamps_ref.at[3 * owner + 2], js_sem.at[1, place], jr_sem.at[1, place], (down, b)),
         )
 
-    start((image_along(0, b, (s, right), masked), image_along(1, b, (s, left), masked)))
-    start(image_across(0, b, masked))
-
-    along(0, left, 0, (s, left)).wait_recv()
-    start((along(4, left, 0, (s, right)),))
-    start(across(1, left, 0))
-    along(2, right, 0, (s, right)).wait_recv()
-    start(across(2, right, 0))
-    along(3, right, 1, (s, right)).wait_recv()
-    start((along(5, right, 1, (s, left)),))
-    start(across(2, right, 1))
-    along(1, left, 1, (s, left)).wait_recv()
-    start(across(1, left, 1))
-
-    image_along(0, left, (s, left), stamps_ref.at[3 * left + 1]).wait_recv()
-    start((image_along(2, left, (s, right), stamps_ref.at[3 * left + 1]),))
-    start(image_across(1, left, stamps_ref.at[3 * left + 1]))
-    image_along(1, right, (s, right), stamps_ref.at[3 * right + 1]).wait_recv()
-    start(image_across(2, right, stamps_ref.at[3 * right + 1]))
-    image_along(2, far, (s, left), stamps_ref.at[3 * far + 1]).wait_recv()
-    start(image_across(3, far, stamps_ref.at[3 * far + 1]))
-
-    along(4, far, 0, (s, left)).wait_recv()
-    start(across(3, far, 0))
-    along(5, far, 1, (s, right)).wait_recv()
-    start(across(3, far, 1))
-
+    sends = []
+
+    def start(*copies):
+        for copy in copies:
+            copy.start()
+        sends.extend(copies)
+
+    start(image_along(0, b, (s, right), masked), image_along(1, b, (s, left), masked))
+    for part in range(4):
+        own = feat_ref.at[PARTS[part]]
+        start(along(0, part, b, part, own), along(1, part, b, 3 - part, feat_ref.at[PARTS[3 - part]]))
+        start(*across(0, b, part, own))
+    start(*image_across(0, b, masked))
+    stamps_ref[3 * b + 1] = masked[...]
+
+    def convert(slot, part, values, blank=None):
+        if blank is not None:
+            values = jnp.where(blank, 0.0, values)
+        rows = PARTS[part]
+        top[slot, rows, :], low[slot, rows, :] = halves(values)
+
+    leaving = []
+
+    def leave(source, out, sem):
+        copy = pltpu.make_async_copy(source, out, sem)
+        copy.start()
+        leaving.append(copy)
+
+    def ship(slot, number):
+        leave(top.at[slot], top_ref.at[slot], out_sem.at[0, number])
+        leave(low.at[slot], low_ref.at[slot], out_sem.at[1, number])
+
+    def settle(place, owner):
+        for part in range(4):
+            for copy in across(place, owner, part):
+                copy.wait_recv()
+            convert(3 * owner, part, window[3 * owner, PARTS[part], :], s == 0)
+            convert(3 * owner + 2, part, window[3 * owner + 2, PARTS[part], :], s == n_sky - 1)
+        ship(3 * owner, 3 * place)
+        ship(3 * owner + 2, 3 * place + 2)
+        for copy in image_across(place, owner, masked):
+            copy.wait_recv()
+        stamps_ref[3 * owner] = jnp.where(s == 0, 0.0, stamps_ref[3 * owner])
+        stamps_ref[3 * owner + 2] = jnp.where(s == n_sky - 1, 0.0, stamps_ref[3 * owner + 2])
+
+    for part in (0, 1):
+        along(0, part, left, part).wait_recv()
+        start(along(0, 4 + part, left, part))
+        start(*across(1, left, part))
+        along(1, part, right, 3 - part).wait_recv()
+        start(along(1, 4 + part, right, 3 - part))
+        start(*across(2, right, 3 - part))
+    image_along(0, left, (s, left), masked).wait_recv()
+    start(image_along(2, left, (s, right), stamps_ref.at[3 * left + 1]))
+    start(*image_across(1, left, stamps_ref.at[3 * left + 1]))
+    image_along(1, right, (s, right), masked).wait_recv()
+    start(*image_across(2, right, stamps_ref.at[3 * right + 1]))
+    fetch_own.wait()
+    for part in range(4):
+        convert(3 * b + 1, part, window[3 * b + 1, PARTS[part], :])
+    ship(3 * b + 1, 1)
+    for part in (2, 3):
+        along(0, part, left, part).wait_recv()
+        start(*across(1, left, part))
+        along(1, part, right, 3 - part).wait_recv()
+        start(*across(2, right, 3 - part))
+    image_along(2, far, (s, left), masked).wait_recv()
+    start(*image_across(3, far, stamps_ref.at[3 * far + 1]))
+    fetch_target.wait()
+    target_top[...], target_low[...] = halves(target[...])
+    leave(target_top, target_top_ref, out_sem.at[0, CAND])
+    leave(target_low, target_low_ref, out_sem.at[1, CAND])
+    for part in (0, 1):
+        along(0, 4 + part, far, part).wait_recv()
+        start(*across(3, far, part))
+        along(1, 4 + part, far, 3 - part).wait_recv()
+        start(*across(3, far, 3 - part))
+    for place, owner in enumerate((left, right, far)):
+        for part in range(4):
+            convert(3 * owner + 1, part, window[3 * owner + 1, PARTS[part], :])
+        ship(3 * owner + 1, 3 * place + 4)
     for place, owner in enumerate((b, left, right, far)):
-        for half in (0, 1):
-            for copy in across(place, owner, half):
-                copy.wait_recv()
-        for copy in image_across(place, owner, stamps_ref.at[3 * owner + 1]):
-            copy.wait_recv()
+        settle(place, owner)
     for copy in sends:
         copy.wait_send()
-    for copy in own:
+    for copy in leaving:
         copy.wait()
 
-    def blank(side):
-        for owner in range(n_batch):
-            copy = pltpu.make_async_copy(zeros, window_ref.at[3 * owner + side], local_sem.at[0])
-            other = pltpu.make_async_copy(zero_image, stamps_ref.at[3 * owner + side], local_sem.at[1])
-            copy.start()
-            other.start()
-            copy.wait()
-            other.wait()
-
-    @pl.when(s == 0)
-    def _():
-        blank(0)
-
-    @pl.when(s == n_sky - 1)
-    def _():
-        blank(2)
-
-
-def gather_window(features, images, layer_mask):
+
+def gather_window(features, images, layer_mask, target):
     n_sky, n_batch = lax.axis_size("sky"), lax.axis_size("batch")
+    vmem, hbm = pl.BlockSpec(memory_space=pltpu.VMEM), pl.BlockSpec(memory_space=pltpu.HBM)
     return pl.pallas_call(
         functools.partial(gather_kernel, n_sky, n_batch),
         out_shape=(
-            jax.ShapeDtypeStruct((CAND, NPIX, FEAT), F32),
+            jax.ShapeDtypeStruct((CAND, NPIX, FEAT), BF16),
+            jax.ShapeDtypeStruct((CAND, NPIX, FEAT), BF16),
             jax.ShapeDtypeStruct((CAND, LAYERS, TILE), F32),
+            jax.ShapeDtypeStruct((NOUT_PIX, FEAT), BF16),
+            jax.ShapeDtypeStruct((NOUT_PIX, FEAT), BF16),
         ),
         in_specs=[
-            pl.BlockSpec(memory_space=pltpu.VMEM),
-            pl.BlockSpec(memory_space=pltpu.VMEM),
+            pl.BlockSpec(memory_space=pltpu.HBM),
+            vmem,
             pl.BlockSpec(memory_space=pltpu.SMEM),
+            pl.BlockSpec(memory_space=pltpu.HBM),
         ],
-        out_specs=(pl.BlockSpec(memory_space=pl.ANY), pl.BlockSpec(memory_space=pl.ANY)),
+        out_specs=(hbm, hbm, vmem, hbm, hbm),
         scratch_shapes=[
+            pltpu.VMEM((CAND, NPIX, FEAT), F32),
+            pltpu.VMEM((NOUT_PIX, FEAT), F32),
             pltpu.VMEM((LAYERS, TILE), F32),
-            pltpu.VMEM((NPIX, FEAT), F32),
-            pltpu.VMEM((LAYERS, TILE), F32),
+            pltpu.VMEM((CAND, NPIX, FEAT), BF16),
+            pltpu.VMEM((CAND, NPIX, FEAT), BF16),
+            pltpu.VMEM((NOUT_PIX, FEAT), BF16),
+            pltpu.VMEM((NOUT_PIX, FEAT), BF16),
             pltpu.SemaphoreType.DMA((2,)),
-            pltpu.SemaphoreType.DMA((6,)),
-            pltpu.SemaphoreType.DMA((6,)),
-            pltpu.SemaphoreType.DMA((2, 8)),
-            pltpu.SemaphoreType.DMA((2, 8)),
+            pltpu.SemaphoreType.DMA((2, CAND + 1)),
+            pltpu.SemaphoreType.DMA((2, 6)),
+            pltpu.SemaphoreType.DMA((2, 6)),
+            pltpu.SemaphoreType.DMA((2, 16)),
+            pltpu.SemaphoreType.DMA((2, 16)),
             pltpu.SemaphoreType.DMA((3,)),
             pltpu.SemaphoreType.DMA((3,)),
             pltpu.SemaphoreType.DMA((2, 4)),
             pltpu.SemaphoreType.DMA((2, 4)),
         ],
-        compiler_params=pltpu.CompilerParams(collective_id=0, has_side_effects=True),
+        compiler_params=pltpu.CompilerParams(
+            collective_id=0, has_side_effects=True, vmem_limit_bytes=60 << 20
+        ),
         name="gather_window",
-    )(features, images, layer_mask)
+    )(features, images, layer_mask, target)
 
 
 def row_of(tile, index):
@@ -304,35 +332,26 @@
     return lax.dot_general(a, b, (dims, ((), ())), precision=HIGH, preferred_element_type=F32)
 
 
-def halves(x):
-    top = x.astype(BF16)
-    return top, (x - top.astype(F32)).astype(BF16)
-
-
 def solve_kernel(
-    pair_ref, ridge_ref, window_ref, stamps_ref, target_ref, transfer_ref, coadd_ref,
-    feats, images, target, feat_top, feat_low, target_top, target_low, system, right,
-    left_top, left_low, across_top, across_low, diag, inverse, previous, sem,
+    pair_ref, ridge_ref, top_ref, low_ref, stamps_ref, target_top_ref, target_low_ref, transfer_ref, coadd_ref,
+    feat_top, feat_low, target_top, target_low, system, right,
+    left_top, left_low, across_top, across_low, column_top, column_low, right_top, right_low, diag, inverse, previous, result, sem,
 ):
     copies = []
     for k in range(NSEL):
-        copies.append(
-            pltpu.make_async_copy(window_ref.at[pair_ref[k]], feats.at[pl.ds(NPIX * k, NPIX)], sem.at[k])
-        )
-    fetch_target = pltpu.make_async_copy(target_ref, target, sem.at[NSEL])
-    for copy in copies:
+        rows = pl.ds(NPIX * k, NPIX)
+        copies.append(pltpu.make_async_copy(top_ref.at[pair_ref[k]], feat_top.at[rows], sem.at[k]))
+        copies.append(pltpu.make_async_copy(low_ref.at[pair_ref[k]], feat_low.at[rows], sem.at[NSEL + k]))
+    later = [
+        pltpu.make_async_copy(target_top_ref, target_top, sem.at[2 * NSEL]),
+        pltpu.make_async_copy(target_low_ref, target_low, sem.at[2 * NSEL + 1]),
+    ]
+    for copy in copies + later:
         copy.start()
-    fetch_images = []
-    for k in range(NSEL):
-        fetch_images.append(pltpu.make_async_copy(stamps_ref.at[pair_ref[k]], images.at[k], sem.at[NSEL + 1 + k]))
-        fetch_images[k].start()
-    fetch_target.start()
     feat_top[ORDER:, :] = jnp.zeros((PADDED - ORDER, FEAT), BF16)
     feat_low[ORDER:, :] = jnp.zeros((PADDED - ORDER, FEAT), BF16)
-    for k in range(NSEL):
-        copies[k].wait()
-        rows = pl.ds(NPIX * k, NPIX)
-        feat_top[rows, :], feat_low[rows, :] = halves(feats[rows, :])
+    for copy in copies:
+        copy.wait()
 
     def product(a_top, a_low, b_top, b_low):
         result = lax.dot_general(a_top, b_top, NT, preferred_element_type=F32)
@@ -356,37 +375,49 @@
         at = pl.ds(TILE * k, TILE)
         system[at, at] += eye
     diag[...] = system[:TILE, :TILE]
-    fetch_target.wait()
-    for copy in fetch_images:
+
+    for copy in later:
         copy.wait()
-
     third = PADDED // 3
+    share = NOUT_PIX // 3
+
+    def block(k):
+        return pl.ds(TILE * k, TILE)
+
+    def product_of_halves(a_top, a_low, b_top, b_low):
+        result = lax.dot_general(
+            jnp.concatenate([a_top, a_low], axis=1), jnp.concatenate([b_top, b_top], axis=1), NT,
+            preferred_element_type=F32,
+        )
+        return result + lax.dot_general(a_top, b_low, NT, preferred_element_type=F32)
+
+    def right_job(part, half):
+        def job():
+            rows, at = pl.ds(share * part, share), pl.ds(PADDED // 2 * half, PADDED // 2)
+            right[rows, at] = product(target_top[rows, :], target_low[rows, :], feat_top[at, :], feat_low[at, :])
+        return job
+
+    def take_job(j):
+        def job():
+            at = block(j)
+            across_top[...], across_low[...] = halves(system[at, :])
+            system[at, :] = jnp.zeros((TILE, PADDED), F32)
+            column_top[...], column_low[...] = halves(system[:, at])
+        return job
 
     def left_job(j, part):
         def job():
-            at = pl.ds(pl.multiple_of(TILE * j, TILE), TILE)
             rows = pl.ds(third * part, third)
-            left = dot(system[rows, at], previous[...])
-            system[rows, at] = -left
+            left = dot(system[rows, block(j)], previous[...])
             left_top[rows, :], left_low[rows, :] = halves(left)
+            if third * part <= TILE * j < third * part + third:
+                left_top[block(j), :], left_low[block(j), :] = halves(-previous[...])
         return job
 
-    def across_job(j):
+    def update_job(j, part):
         def job():
-            at = pl.ds(pl.multiple_of(TILE * j, TILE), TILE)
-            across_top[...], across_low[...] = halves(system[at, :])
-            system[at, :] = jnp.zeros((TILE, PADDED), F32)
-            system[at, at] = previous[...]
-            top, low = halves(-previous[...])
-            left_top[at, :] = top
-            left_low[at, :] = low
-            across_top[:, at] = jnp.zeros((TILE, TILE), BF16)
-            across_low[:, at] = jnp.zeros((TILE, TILE), BF16)
-        return job
-
-    def update_job(part):
-        def job():
-            columns = pl.ds(third * part, third)
+            first = max(third * part, TILE * (j + 1))
+            columns = pl.ds(first, third * part + third - first)
             top = across_top[:, columns]
             change = jnp.dot(
                 jnp.concatenate([left_top[...], left_low[...]], axis=1),
@@ -397,18 +428,19 @@
             system[:, columns] -= change
         return job
 
-    def split_job(part):
+    def scale_job(j):
         def job():
-            rows = pl.ds(NOUT_PIX // 3 * part, NOUT_PIX // 3)
-            target_top[rows, :], target_low[rows, :] = halves(target[rows, :])
+            scaled = dot(right[:, block(j)], previous[...])
+            right[:, block(j)] = scaled
+            right_top[...], right_low[...] = halves(scaled)
         return job
 
-    def right_job(j, part):
+    def right_update_job(j, part):
         def job():
-            at = pl.ds(pl.multiple_of(TILE * j, TILE), TILE)
-            share = NOUT_PIX // 3
-            rows = pl.ds(share * part, share)
-            right[rows, at] = product(target_top[rows, :], target_low[rows, :], feat_top[at, :], feat_low[at, :])
+            columns = pl.ds(third * part, third)
+            right[:, columns] -= product_of_halves(
+                right_top[...], right_low[...], column_top[columns, :], column_low[columns, :]
+            )
         return job
 
     def invert(rows, jobs):
@@ -417,45 +449,52 @@
             inverse[8 * i : 8 * i + 8, :] = group
 
     def advance(k):
-        at = pl.ds(pl.multiple_of(TILE * k, TILE), TILE)
-        then = pl.ds(pl.multiple_of(TILE * k + TILE, TILE), TILE)
+        at, then = block(k), block(k + 1)
         diag[...] = system[then, then] - dot(dot(system[then, at], inverse[...]), system[at, then])
         previous[...] = inverse[...]
 
     def jobs_after(j):
-        return [left_job(j, part) for part in range(3)] + [across_job(j)] + [update_job(part) for part in range(3)]
-
-    invert(TILE, [split_job(part) for part in range(3)] + [right_job(0, part) for part in range(3)])
+        jobs = [take_job(j)] + [left_job(j, part) for part in range(3)]
+        jobs += [update_job(j, part) for part in range(3) if third * part + third > TILE * (j + 1)]
+        return jobs + [scale_job(j)] + [right_update_job(j, part) for part in range(3)]
+
+    invert(TILE, [right_job(part, half) for part in range(3) for half in (0, 1)])
     advance(0)
-
-    def eliminate(k, carry):
-        invert(TILE, jobs_after(k - 1) + [right_job(k, part) for part in range(3)])
+    for k in range(1, NBLOCK - 1):
+        invert(TILE, jobs_after(k - 1))
         advance(k)
-        return carry
-
-    lax.fori_loop(1, NBLOCK - 1, eliminate, 0)
     last = NBLOCK - 1
     inverse[...] = jnp.zeros((TILE, TILE), F32)
-    invert(ORDER - TILE * last, jobs_after(last - 1) + [right_job(last, part) for part in range(3)])
-    previous[...] = inverse[...]
-    for job in jobs_after(last):
-        job()
-    transfer = dot(right[...], system[...])
-    transfer_ref[...] = transfer[:, :ORDER]
+    invert(ORDER - TILE * last, jobs_after(last - 1))
+    column_top[...], column_low[...] = halves(system[:, block(last)])
+    outgoing = []
+    for part in range(3):
+        rows = pl.ds(share * part, share)
+        scaled = dot(right[rows, block(last)], inverse[...])
+        top, low = halves(scaled)
+        head = pl.ds(0, TILE * last)
+        right[rows, head] -= product_of_halves(top, low, column_top[head, :], column_low[head, :])
+        right[rows, block(last)] = scaled
+        result[rows, :] = right[rows, pl.ds(0, ORDER)]
+        copy = pltpu.make_async_copy(result.at[rows], transfer_ref.at[rows], sem.at[part])
+        copy.start()
+        outgoing.append(copy)
 
     empty = jnp.zeros((LAYERS, TILE), F32)
     strips = [empty] * (NBLOCK + 1)
     for k in range(NSEL):
         first, shift = divmod(NPIX * k, TILE)
-        wide = jnp.concatenate([images[k], empty], axis=1)
+        wide = jnp.concatenate([stamps_ref[pair_ref[k]], empty], axis=1)
         if shift:
             wide = pltpu.roll(wide, shift, 1)
         strips[first] = strips[first] + wide[:, :TILE]
         strips[first + 1] = strips[first + 1] + wide[:, TILE:]
-    coadd_ref[...] = dot(jnp.concatenate(strips[:NBLOCK], axis=1), transfer, ((1,), (1,)))
-
-
-def solve(pair_list, ridge, window, stamps, target):
+    coadd_ref[...] = dot(jnp.concatenate(strips[:NBLOCK], axis=1), right[...], ((1,), (1,)))
+    for copy in outgoing:
+        copy.wait()
+
+
+def solve(pair_list, ridge, *arrays):
     return pl.pallas_call(
         solve_kernel,
         out_shape=(
@@ -467,13 +506,12 @@
             pl.BlockSpec(memory_space=pltpu.SMEM),
             pl.BlockSpec(memory_space=pltpu.HBM),
             pl.BlockSpec(memory_space=pltpu.HBM),
+            pl.BlockSpec(memory_space=pltpu.VMEM),
+            pl.BlockSpec(memory_space=pltpu.HBM),
             pl.BlockSpec(memory_space=pltpu.HBM),
         ],
-        out_specs=(pl.BlockSpec(memory_space=pltpu.VMEM), pl.BlockSpec(memory_space=pltpu.VMEM)),
+        out_specs=(pl.BlockSpec(memory_space=pltpu.HBM), pl.BlockSpec(memory_space=pltpu.VMEM)),
         scratch_shapes=[
-            pltpu.VMEM((PADDED, FEAT), F32),
-            pltpu.VMEM((NSEL, LAYERS, TILE), F32),
-            pltpu.VMEM((NOUT_PIX, FEAT), F32),
             pltpu.VMEM((PADDED, FEAT), BF16),
             pltpu.VMEM((PADDED, FEAT), BF16),
             pltpu.VMEM((NOUT_PIX, FEAT), BF16),
@@ -484,14 +522,19 @@
             pltpu.VMEM((PADDED, TILE), BF16),
             pltpu.VMEM((TILE, PADDED), BF16),
             pltpu.VMEM((TILE, PADDED), BF16),
+            pltpu.VMEM((PADDED, TILE), BF16),
+            pltpu.VMEM((PADDED, TILE), BF16),
+            pltpu.VMEM((NOUT_PIX, TILE), BF16),
+            pltpu.VMEM((NOUT_PIX, TILE), BF16),
             pltpu.VMEM((TILE, TILE), F32),
             pltpu.VMEM((TILE, TILE), F32),
             pltpu.VMEM((TILE, TILE), F32),
-            pltpu.SemaphoreType.DMA((2 * NSEL + 1,)),
+            pltpu.VMEM((NOUT_PIX, ORDER), F32),
+            pltpu.SemaphoreType.DMA((2 * NSEL + 2,)),
         ],
-        compiler_params=pltpu.CompilerParams(vmem_limit_bytes=56 << 20),
+        compiler_params=pltpu.CompilerParams(vmem_limit_bytes=60 << 20),
         name="solve_stamp",
-    )(pair_list, ridge, window, stamps, target)
+    )(pair_list, ridge, *arrays)
 
 
 def blend_kernel(n_sky, n_batch, coadd_ref, out_ref, slots, send_sem, recv_sem):
@@ -556,18 +599,19 @@
             pltpu.SemaphoreType.DMA((4,)),
             pltpu.SemaphoreType.DMA((4,)),
         ],
-        compiler_params=pltpu.CompilerParams(collective_id=1, has_side_effects=True),
+        compiler_params=pltpu.CompilerParams(collective_id=1, has_side_effects=True, vmem_limit_bytes=4 << 20),
         name="blend_edges",
     )(coadd)
 
 
 def local(features, target, images, layer_mask, pair_list, ridge_weight):
-    window, stamps = gather_window(
-        features.reshape(NPIX, FEAT), images.reshape(LAYERS, NPIX), layer_mask.reshape(LAYERS)
+    gathered = gather_window(
+        features.reshape(NPIX, FEAT),
+        images.reshape(LAYERS, NPIX),
+        layer_mask.reshape(LAYERS),
+        target.reshape(NOUT_PIX, FEAT),
     )
-    transfer, coadd = solve(
-        pair_list.reshape(NSEL), ridge_weight.reshape(1), window, stamps, target.reshape(NOUT_PIX, FEAT)
-    )
+    transfer, coadd = solve(pair_list.reshape(NSEL), ridge_weight.reshape(1), *gathered)
     final = blend(coadd)
     return (transfer.T.reshape(1, 1, ORDER, NOUT_PIX), final.reshape(LAYERS, SIDE, SIDE))
 

time: 74.8 us -> 70.1 us (0.937)
  Pallas kernels: 71.7 us -> 66.3 us
    pallas_call x1, Pallas kernels: 31.3 us -> 29.2 us  [gather_window(): pl.pallas_call(functools.partial(gather_kernel, n_sky, n_batch), out_shap...]
    pallas_call x1, Pallas kernels: 31.4 us -> 29.4 us  [solve(): pl.pallas_call(solve_kernel, out_shape=(jax.ShapeDtypeStruct((NOUT_PIX, O...]
    pallas_call x1, Pallas kernels: 9.06 us -> 7.72 us  [blend(): pl.pallas_call(functools.partial(blend_kernel, n_sky, n_batch), out_shape...]
    reshape x1, local copies, waits for them, and re-layouts: 1.58 us -> 0.8 us  [local(): final.reshape(LAYERS, SIDE, SIDE)]
    unnamed x0 -> x2, local copies, waits for them, and re-layouts: none -> 0.77 us
where the time goes in v2:
time: 70.1 us; the launch traced here: 69.2 us
  Pallas kernels  66.3 us (95%)
  local copies, waits for them, and re-layouts  1.57 us (2%)
  between operations  1.31 us (2%)
    pallas_call x1, Pallas kernels, solve(): pl.pallas_call(solve_kernel, out_shape=(jax.ShapeDtypeStruct((NOUT_PIX, O...  29.4 us
    pallas_call x1, Pallas kernels, gather_window(): pl.pallas_call(functools.partial(gather_kernel, n_sky, n_batch), out_shap...  29.2 us
    pallas_call x1, Pallas kernels, blend(): pl.pallas_call(functools.partial(blend_kernel, n_sky, n_batch), out_shape...  7.72 us

profile of v2, /device:TPU:6, one launch (start us, length us, event | category | flops | bytes accessed | tf_op | source)
XLA Modules:
  0.0 69.2 jit_solution(11999350982672441088)
XLA Ops:
  1.3 29.2 %gather_window.1 = (bf16[12,80,1024]{2,1,0:T(8,128)(2,1)}, bf16[12,80,1024]{2,1,0:T(8,128)(2,1)}, f32[12,16,128]{2,1,0:T(8,128)}, bf16[576,1024]{1,0:T(8,128)(2,1)}, bf16[576,1024]{1,0:T(8,128)(2,1)}) custom-call(f32[80,1024]{1,0:T(8,128)} %bitcast.11, f32[16,80]{1,0:T(8,128)} %bitcast.12, s32[16]{0:T(128)} %bitcast.13, f32[576,1024]{1,0:T(8,128)} %bitcast.10), custom_call_target="tpu_custom_call" | custom-call | tf_op jit(solution)/shard_map/gather_window/pallas_call | solution.py:186
  30.5 29.4 %solve_stamp.1 = (f32[576,720]{1,0:T(8,128)}, f32[16,576]{1,0:T(8,128)}) custom-call(s32[9]{0:T(128)} %bitcast.14, f32[1]{0:T(128)} %bitcast.9.ridge_ref, bf16[12,80,1024]{2,1,0:T(8,128)(2,1)} %get-tuple-element.9.top_ref, bf16[12,80,1024]{2,1,0:T(8,128)(2,1)} %get-tuple-element.10.low_ref, f32[12,16,128]{2,1,0:T(8,128)} %get-tuple-element.11.stamps_ref, ...), custom_call_target="tpu_custom_call" | custom-call | tf_op jit(solution)/shard_map/solve_stamp/pallas_call | solution.py:498
  59.9 0.0 copy-start
  59.9 0.8 %copy-done = f32[16,576]{1,0:T(8,128)S(1)} copy-done((f32[16,576]{1,0:T(8,128)S(1)}, f32[16,576]{1,0:T(8,128)}, u32[]{:S(2)}) %copy-start) | copy-done | bytes 36888
  60.7 7.7 %blend_edges.1 = f32[16,576]{1,0:T(8,128)S(1)} custom-call(f32[16,576]{1,0:T(8,128)S(1)} %copy-done), custom_call_target="tpu_custom_call" | custom-call | tf_op jit(solution)/shard_map/blend_edges/pallas_call | solution.py:592
  68.4 0.8 %reshape.35 = f32[16,24,24]{2,1,0:T(8,128)} reshape(f32[16,576]{1,0:T(8,128)S(1)} %blend_edges.1) | data formatting | bytes 73728 | tf_op jit(solution)/shard_map/reshape | solution.py:616
Async XLA Ops:
  59.9 0.8 %copy-start = (f32[16,576]{1,0:T(8,128)S(1)}, f32[16,576]{1,0:T(8,128)}, u32[]{:S(2)}) copy-start(f32[16,576]{1,0:T(8,128)} %get-tuple-element.15.coadd_ref) | copy-start | bytes 110596

commit v3 on v2

--- a/solution.py
+++ b/solution.py
@@ -391,12 +391,6 @@
         )
         return result + lax.dot_general(a_top, b_low, NT, preferred_element_type=F32)
 
-    def right_job(part, half):
-        def job():
-            rows, at = pl.ds(share * part, share), pl.ds(PADDED // 2 * half, PADDED // 2)
-            right[rows, at] = product(target_top[rows, :], target_low[rows, :], feat_top[at, :], feat_low[at, :])
-        return job
-
     def take_job(j):
         def job():
             at = block(j)
@@ -454,11 +448,12 @@
         previous[...] = inverse[...]
 
     def jobs_after(j):
-        jobs = [take_job(j)] + [left_job(j, part) for part in range(3)]
+        jobs = [take_job(j), scale_job(j)] + [left_job(j, part) for part in range(3)]
         jobs += [update_job(j, part) for part in range(3) if third * part + third > TILE * (j + 1)]
-        return jobs + [scale_job(j)] + [right_update_job(j, part) for part in range(3)]
-
-    invert(TILE, [right_job(part, half) for part in range(3) for half in (0, 1)])
+        return jobs + [right_update_job(j, part) for part in range(3)]
+
+    right[...] = product(target_top[...], target_low[...], feat_top[...], feat_low[...])
+    invert(TILE, [])
     advance(0)
     for k in range(1, NBLOCK - 1):
         invert(TILE, jobs_after(k - 1))

time: 70.1 us -> 68.8 us (0.981)
  Pallas kernels: 66.3 us -> 65 us
    pallas_call x1, Pallas kernels: 29.4 us -> 28.1 us  [solve(): pl.pallas_call(solve_kernel, out_shape=(jax.ShapeDtypeStruct((NOUT_PIX, O...]
where the time goes in v3:
time: 68.8 us; the launch traced here: 67.9 us
  Pallas kernels  65 us (94%)
  local copies, waits for them, and re-layouts  1.57 us (2%)
  between operations  1.31 us (2%)
    pallas_call x1, Pallas kernels, gather_window(): pl.pallas_call(functools.partial(gather_kernel, n_sky, n_batch), out_shap...  29.2 us
    pallas_call x1, Pallas kernels, solve(): pl.pallas_call(solve_kernel, out_shape=(jax.ShapeDtypeStruct((NOUT_PIX, O...  28.1 us
    pallas_call x1, Pallas kernels, blend(): pl.pallas_call(functools.partial(blend_kernel, n_sky, n_batch), out_shape...  7.72 us

profile of v3, /device:TPU:6, one launch (start us, length us, event | category | flops | bytes accessed | tf_op | source)
XLA Modules:
  0.0 67.9 jit_solution(8146787814518841042)
XLA Ops:
  1.3 29.2 %gather_window.1 = (bf16[12,80,1024]{2,1,0:T(8,128)(2,1)}, bf16[12,80,1024]{2,1,0:T(8,128)(2,1)}, f32[12,16,128]{2,1,0:T(8,128)}, bf16[576,1024]{1,0:T(8,128)(2,1)}, bf16[576,1024]{1,0:T(8,128)(2,1)}) custom-call(f32[80,1024]{1,0:T(8,128)} %bitcast.11, f32[16,80]{1,0:T(8,128)} %bitcast.12, s32[16]{0:T(128)} %bitcast.13, f32[576,1024]{1,0:T(8,128)} %bitcast.10), custom_call_target="tpu_custom_call" | custom-call | tf_op jit(solution)/shard_map/gather_window/pallas_call | solution.py:186
  30.5 28.1 %solve_stamp.1 = (f32[576,720]{1,0:T(8,128)}, f32[16,576]{1,0:T(8,128)}) custom-call(s32[9]{0:T(128)} %bitcast.14, f32[1]{0:T(128)} %bitcast.9.ridge_ref, bf16[12,80,1024]{2,1,0:T(8,128)(2,1)} %get-tuple-element.9.top_ref, bf16[12,80,1024]{2,1,0:T(8,128)(2,1)} %get-tuple-element.10.low_ref, f32[12,16,128]{2,1,0:T(8,128)} %get-tuple-element.11.stamps_ref, ...), custom_call_target="tpu_custom_call" | custom-call | tf_op jit(solution)/shard_map/solve_stamp/pallas_call | solution.py:493
  58.6 0.0 copy-start
  58.6 0.8 %copy-done = f32[16,576]{1,0:T(8,128)S(1)} copy-done((f32[16,576]{1,0:T(8,128)S(1)}, f32[16,576]{1,0:T(8,128)}, u32[]{:S(2)}) %copy-start) | copy-done | bytes 36888
  59.4 7.7 %blend_edges.1 = f32[16,576]{1,0:T(8,128)S(1)} custom-call(f32[16,576]{1,0:T(8,128)S(1)} %copy-done), custom_call_target="tpu_custom_call" | custom-call | tf_op jit(solution)/shard_map/blend_edges/pallas_call | solution.py:587
  67.1 0.8 %reshape.35 = f32[16,24,24]{2,1,0:T(8,128)} reshape(f32[16,576]{1,0:T(8,128)S(1)} %blend_edges.1) | data formatting | bytes 73728 | tf_op jit(solution)/shard_map/reshape | solution.py:611
Async XLA Ops:
  58.6 0.8 %copy-start = (f32[16,576]{1,0:T(8,128)S(1)}, f32[16,576]{1,0:T(8,128)}, u32[]{:S(2)}) copy-start(f32[16,576]{1,0:T(8,128)} %get-tuple-element.15.coadd_ref) | copy-start | bytes 110596

commit v4 on v3

--- a/solution.py
+++ b/solution.py
@@ -20,7 +20,7 @@
 TILE = 128
 NBLOCK = 6
 PADDED = TILE * NBLOCK
-PARTS = (pl.ds(0, 24), pl.ds(24, 16), pl.ds(40, 24), pl.ds(64, 16))
+PARTS = (pl.ds(0, 40), pl.ds(40, 40))
 MESH = pl.DeviceIdType.MESH
 HIGH = lax.Precision.HIGH
 NT = (((1,), (1,)), ((), ()))
@@ -76,7 +76,7 @@
 
     def across(place, owner, part, src=None):
         base = window.at[3 * owner + 1, PARTS[part]] if src is None else src
-        number = 4 * place + part
+        number = 2 * place + part
         return (
             remote(base, window.at[3 * owner, PARTS[part]], ys_sem.at[0, number], yr_sem.at[0, number], (up, b)),
             remote(base, window.at[3 * owner + 2, PARTS[part]], ys_sem.at[1, number], yr_sem.at[1, number], (down, b)),
@@ -99,18 +99,18 @@
         sends.extend(copies)
 
     start(image_along(0, b, (s, right), masked), image_along(1, b, (s, left), masked))
-    for part in range(4):
+    for part in range(2):
         own = feat_ref.at[PARTS[part]]
-        start(along(0, part, b, part, own), along(1, part, b, 3 - part, feat_ref.at[PARTS[3 - part]]))
+        start(along(0, part, b, part, own), along(1, part, b, 1 - part, feat_ref.at[PARTS[1 - part]]))
         start(*across(0, b, part, own))
     start(*image_across(0, b, masked))
     stamps_ref[3 * b + 1] = masked[...]
 
-    def convert(slot, part, values, blank=None):
+    def convert(slot, blank=None):
+        values = window[slot]
         if blank is not None:
             values = jnp.where(blank, 0.0, values)
-        rows = PARTS[part]
-        top[slot, rows, :], low[slot, rows, :] = halves(values)
+        top[slot], low[slot] = halves(values)
 
     leaving = []
 
@@ -124,11 +124,11 @@
         leave(low.at[slot], low_ref.at[slot], out_sem.at[1, number])
 
     def settle(place, owner):
-        for part in range(4):
+        for part in range(2):
             for copy in across(place, owner, part):
                 copy.wait_recv()
-            convert(3 * owner, part, window[3 * owner, PARTS[part], :], s == 0)
-            convert(3 * owner + 2, part, window[3 * owner + 2, PARTS[part], :], s == n_sky - 1)
+        convert(3 * owner, s == 0)
+        convert(3 * owner + 2, s == n_sky - 1)
         ship(3 * owner, 3 * place)
         ship(3 * owner + 2, 3 * place + 2)
         for copy in image_across(place, owner, masked):
@@ -136,41 +136,39 @@
         stamps_ref[3 * owner] = jnp.where(s == 0, 0.0, stamps_ref[3 * owner])
         stamps_ref[3 * owner + 2] = jnp.where(s == n_sky - 1, 0.0, stamps_ref[3 * owner + 2])
 
-    for part in (0, 1):
+    for part in (0,):
         along(0, part, left, part).wait_recv()
-        start(along(0, 4 + part, left, part))
+        start(along(0, 2 + part, left, part))
         start(*across(1, left, part))
-        along(1, part, right, 3 - part).wait_recv()
-        start(along(1, 4 + part, right, 3 - part))
-        start(*across(2, right, 3 - part))
+        along(1, part, right, 1 - part).wait_recv()
+        start(along(1, 2 + part, right, 1 - part))
+        start(*across(2, right, 1 - part))
     image_along(0, left, (s, left), masked).wait_recv()
     start(image_along(2, left, (s, right), stamps_ref.at[3 * left + 1]))
     start(*image_across(1, left, stamps_ref.at[3 * left + 1]))
     image_along(1, right, (s, right), masked).wait_recv()
     start(*image_across(2, right, stamps_ref.at[3 * right + 1]))
     fetch_own.wait()
-    for part in range(4):
-        convert(3 * b + 1, part, window[3 * b + 1, PARTS[part], :])
+    convert(3 * b + 1)
     ship(3 * b + 1, 1)
-    for part in (2, 3):
+    for part in (1,):
         along(0, part, left, part).wait_recv()
         start(*across(1, left, part))
-        along(1, part, right, 3 - part).wait_recv()
-        start(*across(2, right, 3 - part))
+        along(1, part, right, 1 - part).wait_recv()
+        start(*across(2, right, 1 - part))
     image_along(2, far, (s, left), masked).wait_recv()
     start(*image_across(3, far, stamps_ref.at[3 * far + 1]))
     fetch_target.wait()
     target_top[...], target_low[...] = halves(target[...])
     leave(target_top, target_top_ref, out_sem.at[0, CAND])
     leave(target_low, target_low_ref, out_sem.at[1, CAND])
-    for part in (0, 1):
-        along(0, 4 + part, far, part).wait_recv()
+    for part in (0,):
+        along(0, 2 + part, far, part).wait_recv()
         start(*across(3, far, part))
-        along(1, 4 + part, far, 3 - part).wait_recv()
-        start(*across(3, far, 3 - part))
+        along(1, 2 + part, far, 1 - part).wait_recv()
+        start(*across(3, far, 1 - part))
     for place, owner in enumerate((left, right, far)):
-        for part in range(4):
-            convert(3 * owner + 1, part, window[3 * owner + 1, PARTS[part], :])
+        convert(3 * owner + 1)
         ship(3 * owner + 1, 3 * place + 4)
     for place, owner in enumerate((b, left, right, far)):
         settle(place, owner)
@@ -209,10 +207,10 @@
             pltpu.VMEM((NOUT_PIX, FEAT), BF16),
             pltpu.SemaphoreType.DMA((2,)),
             pltpu.SemaphoreType.DMA((2, CAND + 1)),
-            pltpu.SemaphoreType.DMA((2, 6)),
-            pltpu.SemaphoreType.DMA((2, 6)),
-            pltpu.SemaphoreType.DMA((2, 16)),
-            pltpu.SemaphoreType.DMA((2, 16)),
+            pltpu.SemaphoreType.DMA((2, 3)),
+            pltpu.SemaphoreType.DMA((2, 3)),
+            pltpu.SemaphoreType.DMA((2, 8)),
+            pltpu.SemaphoreType.DMA((2, 8)),
             pltpu.SemaphoreType.DMA((3,)),
             pltpu.SemaphoreType.DMA((3,)),
             pltpu.SemaphoreType.DMA((2, 4)),

time: 68.8 us -> 68.5 us (level)
    pallas_call x1, Pallas kernels: 7.72 us -> 8.41 us  [blend(): pl.pallas_call(functools.partial(blend_kernel, n_sky, n_batch), out_shape...]
where the time goes in v4:
time: 68.5 us; the launch traced here: 68.3 us
  Pallas kernels  65.4 us (95%)
  local copies, waits for them, and re-layouts  1.57 us (2%)
  between operations  1.31 us (2%)
    pallas_call x1, Pallas kernels, gather_window(): pl.pallas_call(functools.partial(gather_kernel, n_sky, n_batch), out_shap...  28.9 us
    pallas_call x1, Pallas kernels, solve(): pl.pallas_call(solve_kernel, out_shape=(jax.ShapeDtypeStruct((NOUT_PIX, O...  28.1 us
    pallas_call x1, Pallas kernels, blend(): pl.pallas_call(functools.partial(blend_kernel, n_sky, n_batch), out_shape...  8.41 us

profile of v4, /device:TPU:6, one launch (start us, length us, event | category | flops | bytes accessed | tf_op | source)
XLA Modules:
  0.0 68.3 jit_solution(11885359763813894630)
XLA Ops:
  1.3 28.9 %gather_window.1 = (bf16[12,80,1024]{2,1,0:T(8,128)(2,1)}, bf16[12,80,1024]{2,1,0:T(8,128)(2,1)}, f32[12,16,128]{2,1,0:T(8,128)}, bf16[576,1024]{1,0:T(8,128)(2,1)}, bf16[576,1024]{1,0:T(8,128)(2,1)}) custom-call(f32[80,1024]{1,0:T(8,128)} %bitcast.11, f32[16,80]{1,0:T(8,128)} %bitcast.12, s32[16]{0:T(128)} %bitcast.13, f32[576,1024]{1,0:T(8,128)} %bitcast.10), custom_call_target="tpu_custom_call" | custom-call | tf_op jit(solution)/shard_map/gather_window/pallas_call | solution.py:184
  30.1 28.1 %solve_stamp.1 = (f32[576,720]{1,0:T(8,128)}, f32[16,576]{1,0:T(8,128)}) custom-call(s32[9]{0:T(128)} %bitcast.14, f32[1]{0:T(128)} %bitcast.9.ridge_ref, bf16[12,80,1024]{2,1,0:T(8,128)(2,1)} %get-tuple-element.9.top_ref, bf16[12,80,1024]{2,1,0:T(8,128)(2,1)} %get-tuple-element.10.low_ref, f32[12,16,128]{2,1,0:T(8,128)} %get-tuple-element.11.stamps_ref, ...), custom_call_target="tpu_custom_call" | custom-call | tf_op jit(solution)/shard_map/solve_stamp/pallas_call | solution.py:491
  58.3 0.0 copy-start
  58.3 0.8 %copy-done = f32[16,576]{1,0:T(8,128)S(1)} copy-done((f32[16,576]{1,0:T(8,128)S(1)}, f32[16,576]{1,0:T(8,128)}, u32[]{:S(2)}) %copy-start) | copy-done | bytes 36888
  59.1 8.4 %blend_edges.1 = f32[16,576]{1,0:T(8,128)S(1)} custom-call(f32[16,576]{1,0:T(8,128)S(1)} %copy-done), custom_call_target="tpu_custom_call" | custom-call | tf_op jit(solution)/shard_map/blend_edges/pallas_call | solution.py:585
  67.5 0.8 %reshape.35 = f32[16,24,24]{2,1,0:T(8,128)} reshape(f32[16,576]{1,0:T(8,128)S(1)} %blend_edges.1) | data formatting | bytes 73728 | tf_op jit(solution)/shard_map/reshape | solution.py:609
Async XLA Ops:
  58.3 0.8 %copy-start = (f32[16,576]{1,0:T(8,128)S(1)}, f32[16,576]{1,0:T(8,128)}, u32[]{:S(2)}) copy-start(f32[16,576]{1,0:T(8,128)} %get-tuple-element.15.coadd_ref) | copy-start | bytes 110596
